TPU v7x, 256 devices: a whole 4x4x8 slice. The times are simulated.
256 devices in a mesh: train: 32 (over y_hi, z, core), cand: 8 (over x, y_lo).
Axes of the slice: x: 4, y: 4 (y_hi: 2, y_lo: 2; y = y_hi * 2 + y_lo), z: 8, core: 2. Of those that a mesh axis runs over, the one named last changes fastest.
Arguments:
- x_train: float32 [8, 16384], P(None, 'train'), may hold values from -4 to 4
- x_cand: float32 [8, 8192], P(None, 'cand'), may hold values from -4 to 4
- targets: float32 [16384], P(('train', 'cand')), may hold values from -6 to 6
- noise: float32 [16384, 64], P(('train', 'cand')), may hold values from -5 to 5
- omega: float32 [8, 4096], replicated, may hold values from -6 to 6
- phase: float32 [4096], replicated, may hold values from -3.140625 to 3.140625
- prior_weights: bfloat16 [4096, 64], P('cand'), may hold values from -6 to 6
Outputs:
- samples: float32 [8192, 64], P(('cand', 'train'))
- solution: float32 [16384, 64], P(('train', 'cand'))
All inputs are finite; a program needn't handle non-finite values.
Results may differ from a plain program's by a relative error of at most 0.0019.
The roundings to bfloat16 on the way count: a program that leaves them out, or rounds other values in their place, can miss the bound.
Values may be sent and summed in bfloat16 or wider, within the bound.
A program may use at most 64 MiB of HBM per device.

v0:
```python
import math
import jax
import jax.numpy as jnp
from jax import lax
from jax.sharding import PartitionSpec as P

ITERS = 2
noise_level = 0.5


def squares_of(points):
    return jnp.sum(points * points, axis=0)


def kernel_tile(row_points, row_norms, column_points, column_norms):
    inner = jnp.dot(row_points.T, column_points, precision=lax.Precision.HIGHEST)
    return jnp.exp(-0.5 * (row_norms[:, None] + column_norms[None, :] - 2.0 * inner)).astype(
        jnp.bfloat16
    )


def features(points, omega, phase):
    angles = jnp.dot(points.T, omega, precision=lax.Precision.HIGHEST) + phase[None, :]
    return (math.sqrt(2.0 / omega.shape[1]) * jnp.cos(angles)).astype(jnp.bfloat16)


def kernel_rows(points, every_point, every_norm, weights):
    count = points.shape[1]
    size = math.gcd(count, 1024)
    stacked = points.reshape(points.shape[0], count // size, size).transpose(1, 0, 2)

    def one_block(block_points):
        tile = kernel_tile(block_points, squares_of(block_points), every_point, every_norm)
        return jnp.dot(tile, weights, preferred_element_type=jnp.float32)

    return lax.map(one_block, stacked).reshape(count, weights.shape[1])


def body(x_train, x_cand, targets, noise, omega, phase, prior_weights):
    own_rows = noise.shape[0]
    cand_index = lax.axis_index("cand")
    train_index = lax.axis_index("train")
    own_points = lax.dynamic_slice_in_dim(x_train, cand_index * own_rows, own_rows, 1)
    full_weights = lax.all_gather(prior_weights, "cand", axis=0, tiled=True)
    prior_train = jnp.dot(
        features(own_points, omega, phase), full_weights, preferred_element_type=jnp.float32
    )
    rhs = targets[:, None] - prior_train - noise
    column_points = lax.all_gather(x_train, "train", axis=1, tiled=True)
    row_norms = squares_of(own_points)
    column_norms = squares_of(column_points)
    width = max(128, 262144 // own_points.shape[1])

    def squares(values):
        return lax.psum(jnp.sum(values * values, axis=0), ("train", "cand"))

    solution = jnp.zeros(rhs.shape, jnp.float32)
    residual = rhs
    direction = rhs
    norm_now = squares(residual)
    for step in range(ITERS):
        packed = direction.astype(jnp.bfloat16)
        empty = jnp.zeros((own_points.shape[1], packed.shape[1]), jnp.float32)
        total = empty
        piece = lax.all_gather(packed, ("train", "cand"), axis=0, tiled=True)
        for offset in range(0, piece.shape[0], width):
            count = min(width, piece.shape[0] - offset)
            accumulate_points = lax.dynamic_slice_in_dim(column_points, offset, count, 1)
            norms = lax.dynamic_slice_in_dim(column_norms, offset, count, 0)
            tile = kernel_tile(own_points, row_norms, accumulate_points, norms)
            total = total + jnp.dot(
                tile, piece[offset : offset + count], preferred_element_type=jnp.float32
            )
        image = total + noise_level * direction
        curve = lax.psum(jnp.sum(direction * image, axis=0), ("train", "cand"))
        alpha = norm_now / curve
        solution = solution + alpha * direction
        residual = residual - alpha * image
        norm_next = squares(residual)
        direction = residual + norm_next / norm_now * direction
        norm_now = norm_next
    per_device = x_cand.shape[1] // lax.axis_size("train")
    mine = lax.dynamic_slice_in_dim(x_cand, train_index * per_device, per_device, 1)
    packed_solution = solution.astype(jnp.bfloat16)
    block_weights = lax.all_gather(packed_solution, "cand", axis=0, tiled=True)
    train_norms = squares_of(x_train)
    kernel_part = lax.psum_scatter(
        kernel_rows(x_cand, x_train, train_norms, block_weights),
        "train",
        scatter_dimension=0,
        tiled=True,
    )
    prior_cand = jnp.dot(
        features(mine, omega, phase), full_weights, preferred_element_type=jnp.float32
    )
    return (prior_cand + kernel_part, solution)


def solution(mesh):
    placed = (
        P(None, "train"),
        P(None, "cand"),
        P(("train", "cand")),
        P(("train", "cand"), None),
        P(),
        P(),
        P("cand", None),
    )
    return jax.shard_map(
        body,
        mesh=mesh,
        in_specs=placed,
        out_specs=(P(("cand", "train"), None), P(("train", "cand"), None)),
        check_vma=False,
    )
```

profile of v0, /device:TPU:4, one launch (start us, length us, event | category | flops | bytes accessed | tf_op | source)
XLA Modules:
  0.0 1849.0 jit_solution(14359610649674526647)
XLA Ops:
  7.2 27.6 %all_gather.15 = bf16[4096,64]{0,1:T(8,128)(2,1)S(1)} all-gather(bf16[512,64]{0,1:T(8,128)(2,1)} %param.13), channel_id=1, replica_groups=mesh['train'=32,'cand'=8] {'cand'}, dimensions={0}, use_global_device_ids=true | all-gather | bytes 589824 | tf_op jit(solution)/shard_map/all_gather | solution.py:44
  34.9 5.5 fusion.14
  40.3 1.7 fusion.56
  42.9 44.9 %all_gather.16 = f32[8,16384]{1,0:T(8,128)S(1)} all-gather(f32[8,512]{1,0:T(8,128)} %param.7), channel_id=1, replica_groups=mesh['train'=32,'cand'=8] {'train'}, dimensions={1}, use_global_device_ids=true | all-gather | bytes 540672 | tf_op jit(solution)/shard_map/all_gather | solution.py:49
  87.9 2.0 fusion.15
  91.2 1.3 fusion.17
  93.7 654.8 %all-gather.3.cloned.1.call-done = bf16[16384,64]{1,0:T(8,128)(2,1)} async-done(((bf16[64,64]{1,0:T(8,128)(2,1)}), bf16[16384,64]{1,0:T(8,128)(2,1)}) %all-gather.3.cloned.1.call-update) | async-done | bytes 2097168 | tf_op jit(solution)/shard_map/all_gather | solution.py:65
  748.5 1.5 fusion.35
  750.1 1.5 convolution_add_fusion.7
  751.6 1.5 convolution_add_fusion.6
  753.2 1.6 multiply_reduce_fusion.2
  754.7 82.4 %all-reduce = (f32[64]{0:T(128)S(1)}, f32[64]{0:T(128)S(1)}) all-reduce(f32[64]{0:T(128)S(1)} %get-tuple-element.15, f32[64]{0:T(128)S(1)} %get-tuple-element.14), channel_id=1, replica_groups=mesh['train'=32,'cand'=8] {'train','cand'}, use_global_device_ids=true, to_apply=%region_3.0 | all-reduce | flops 128 | bytes 1024 | tf_op jit(solution)/shard_map/psum | solution.py:55
  837.2 72.7 %psum.30 = f32[64]{0:T(128)S(1)} all-reduce(f32[64]{0:T(128)S(1)} %multiply_reduce_fusion.1), channel_id=1, replica_groups=mesh['train'=32,'cand'=8] {'train','cand'}, use_global_device_ids=true, to_apply=%region_9.0 | all-reduce | flops 64 | bytes 512 | tf_op jit(solution)/shard_map/psum | solution.py:55
  910.8 2.2 exponential_convert_fusion
  913.0 698.1 %all-gather.5.cloned.1.call-done = bf16[16384,64]{1,0:T(8,128)(2,1)} async-done(((bf16[64,64]{1,0:T(8,128)(2,1)}), bf16[16384,64]{1,0:T(8,128)(2,1)}) %all-gather.5.cloned.1.call-update) | async-done | bytes 2097168 | tf_op jit(solution)/shard_map/all_gather | solution.py:65
  1611.1 1.7 fusion.30
  1612.8 1.5 convolution_add_fusion.4
  1614.4 1.5 convolution_add_fusion.3
  1615.9 1.6 fusion.26
  1617.5 82.4 %psum.31 = f32[64]{0:T(128)S(1)} all-reduce(f32[64]{0:T(128)S(1)} %fusion.26), channel_id=1, replica_groups=mesh['train'=32,'cand'=8] {'train','cand'}, use_global_device_ids=true, to_apply=%region_11.12 | all-reduce | flops 64 | bytes 512 | tf_op jit(solution)/shard_map/psum | solution.py:75
  1700.5 26.1 %all_gather.19 = bf16[512,64]{1,0:T(8,128)(2,1)S(1)} all-gather(bf16[64,64]{1,0:T(8,128)(2,1)S(1)} %get-tuple-element.24), channel_id=1, replica_groups=mesh['train'=32,'cand'=8] {'cand'}, dimensions={0}, use_global_device_ids=true | all-gather | bytes 73728 | tf_op jit(solution)/shard_map/all_gather | solution.py:85
  1727.8 2.7 fusion.21
  1730.5 110.3 %reduce-scatter.2.cloned.1.call-done = f32[32,64]{1,0:T(8,128)} async-done(((f32[1024,64]{1,0:T(8,128)}), f32[32,64]{1,0:T(8,128)}) %reduce-scatter.2.cloned.1.call-update) | async-done | bytes 8208 | tf_op jit(solution)/shard_map/reduce_scatter | solution.py:87
  1840.8 1.6 convolution_add_fusion.8
  (30 shorter events, 6.4 us)
Async XLA Ops:
  7.2 27.7 %copy-start = (f32[8,4096]{1,0:T(8,128)S(1)}, f32[8,4096]{1,0:T(8,128)}, u32[]{:S(2)}) copy-start(f32[8,4096]{1,0:T(8,128)} %param.11) | copy-start | bytes 393220
  7.2 82.7 %copy-start.1 = (f32[8,512]{1,0:T(8,128)S(1)}, f32[8,512]{1,0:T(8,128)}, u32[]{:S(2)}) copy-start(f32[8,512]{1,0:T(8,128)} %param.7) | copy-start | bytes 49156
  7.2 741.3 %all-gather.3.cloned.1.call-start = ((), (), s32[]{:S(2)}) async-start(), calls=%async_computation.1 | async-start | bytes 4210688 | tf_op jit(solution)/shard_map/all_gather | solution.py:65
  42.1 1569.1 %all-gather.5.cloned.1.call-start = ((), (), s32[]{:S(2)}) async-start(), calls=%async_computation.2 | async-start | bytes 4210688 | tf_op jit(solution)/shard_map/all_gather | solution.py:65
  92.4 818.4 %copy-start.3 = (f32[8,1024]{1,0:T(8,128)S(1)}, f32[8,1024]{1,0:T(8,128)}, u32[]{:S(2)}) copy-start(f32[8,1024]{1,0:T(8,128)} %param.8) | copy-start | bytes 98308
  93.7 659.5 %copy-start.4 = (bf16[64,4096]{1,0:T(8,128)(2,1)}, bf16[64,4096]{1,0:T(8,128)(2,1)S(1)}, u32[]{:S(2)}) copy-start(bf16[64,4096]{1,0:T(8,128)(2,1)S(1)} %fusion.18) | copy-start | bytes 1572868
  910.5 930.3 %reduce-scatter.2.cloned.1.call-start = ((), (), s32[]{:S(2)}) async-start(), calls=%async_computation.3 | async-start | bytes 540672 | tf_op jit(solution)/shard_map/reduce_scatter | solution.py:87
  913.0 814.8 %copy-start.2 = (f32[4096]{0:T(1024)S(1)}, f32[4096]{0:T(1024)}, u32[]{:S(2)}) copy-start(f32[4096]{0:T(1024)} %param.12) | copy-start | bytes 49156
Sparse Core Ops, SparseCore 0:
  42.2 706.2 all-gather.2
  910.7 700.4 all-gather.4
  1727.9 112.8 reduce-scatter.1
where the time goes:
time: 1850 us
  waiting for transfers between devices  1460 us (79%)
  blocking collectives  336 us (18%)
  matrix products  33.1 us (2%)
    all_gather x2, waiting for transfers between devices, body(): piece = lax.all_gather(packed, ('train', 'cand'), axis=0, tiled=True)  1350 us
    psum x2, blocking collectives, squares(): return lax.psum(jnp.sum(values * values, axis=0), ('train', 'cand'))  155 us
    reduce_scatter x1, waiting for transfers between devices, body(): lax.psum_scatter(kernel_rows(x_cand, x_train, train_norms, block_weights)...  110 us
    psum x1, blocking collectives, body(): curve = lax.psum(jnp.sum(direction * image, axis=0), ('train', 'cand'))  82.4 us
    all_gather x1, blocking collectives, body(): column_points = lax.all_gather(x_train, 'train', axis=1, tiled=True)  44.9 us
  transfers between devices with their start and end apart: 3, of which 3 were waited for; matrix products, arithmetic and copies ran while one was open for 1% of the time, Pallas kernels for 0%

commit v1 on v0

--- a/solution.py
+++ b/solution.py
@@ -1,3 +1,4 @@
+import functools
 import math
 import jax
 import jax.numpy as jnp
@@ -6,6 +7,15 @@
 
 ITERS = 2
 noise_level = 0.5
+
+
+def process_the_screen(patch, link_axis, mesh_dim):
+    for q in (link_axis, mesh_dim):
+        patch = lax.psum(patch, q)
+    return patch
+
+
+use_field = functools.partial(process_the_screen, link_axis="cand", mesh_dim="train")
 
 
 def squares_of(points):
@@ -72,7 +82,7 @@
                 tile, piece[offset : offset + count], preferred_element_type=jnp.float32
             )
         image = total + noise_level * direction
-        curve = lax.psum(jnp.sum(direction * image, axis=0), ("train", "cand"))
+        curve = use_field(jnp.sum(direction * image, axis=0))
         alpha = norm_now / curve
         solution = solution + alpha * direction
         residual = residual - alpha * image

time: 1850 us -> 1930 us (1.043)
  blocking collectives: 336 us -> 416 us
    psum x1 -> x4, blocking collectives: 82.4 us -> 165 us  [process_the_screen(): patch = lax.psum(patch, q)]
where the time goes in v1:
time: 1930 us
  waiting for transfers between devices  1460 us (76%)
  blocking collectives  416 us (22%)
  matrix products  33.1 us (2%)
    all_gather x2, waiting for transfers between devices, body(): piece = lax.all_gather(packed, ('train', 'cand'), axis=0, tiled=True)  1350 us
    psum x4, blocking collectives, process_the_screen(): patch = lax.psum(patch, q)  165 us
    psum x2, blocking collectives, squares(): return lax.psum(jnp.sum(values * values, axis=0), ('train', 'cand'))  149 us
    reduce_scatter x1, waiting for transfers between devices, body(): lax.psum_scatter(kernel_rows(x_cand, x_train, train_norms, block_weights)...  109 us
    all_gather x1, blocking collectives, body(): column_points = lax.all_gather(x_train, 'train', axis=1, tiled=True)  44.9 us
  transfers between devices with their start and end apart: 3, of which 3 were waited for; matrix products, arithmetic and copies ran while one was open for 1% of the time, Pallas kernels for 0%

profile of v1, /device:TPU:4, one launch (start us, length us, event | category | flops | bytes accessed | tf_op | source)
XLA Modules:
  0.0 1925.2 jit_solution(1339160358012722873)
XLA Ops:
  7.2 27.6 %all_gather.15 = bf16[4096,64]{0,1:T(8,128)(2,1)S(1)} all-gather(bf16[512,64]{0,1:T(8,128)(2,1)} %param.13), channel_id=1, replica_groups=mesh['train'=32,'cand'=8] {'cand'}, dimensions={0}, use_global_device_ids=true | all-gather | bytes 589824 | tf_op jit(solution)/shard_map/all_gather | solution.py:54
  34.9 5.5 fusion.14
  40.3 1.7 fusion.56
  42.9 44.9 %all_gather.16 = f32[8,16384]{1,0:T(8,128)S(1)} all-gather(f32[8,512]{1,0:T(8,128)} %param.7), channel_id=1, replica_groups=mesh['train'=32,'cand'=8] {'train'}, dimensions={1}, use_global_device_ids=true | all-gather | bytes 540672 | tf_op jit(solution)/shard_map/all_gather | solution.py:59
  87.9 2.0 fusion.15
  93.7 654.8 %all-gather.3.cloned.1.call-done = bf16[16384,64]{1,0:T(8,128)(2,1)} async-done(((bf16[64,64]{1,0:T(8,128)(2,1)}), bf16[16384,64]{1,0:T(8,128)(2,1)}) %all-gather.3.cloned.1.call-update) | async-done | bytes 2097168 | tf_op jit(solution)/shard_map/all_gather | solution.py:75
  750.1 1.5 convolution_add_fusion.7
  751.6 1.5 convolution_add_fusion.6
  753.2 1.6 multiply_reduce_fusion.2
  754.7 17.7 psum.43
  772.4 65.0 %psum.44 = f32[64]{0:T(128)S(1)} all-reduce(f32[64]{0:T(128)S(1)} %psum.43), channel_id=1, replica_groups=mesh['train'=32,'cand'=8] {'train'}, use_global_device_ids=true, to_apply=%region_8.0 | all-reduce | flops 64 | bytes 512 | tf_op jit(solution)/shard_map/psum | solution.py:14
  837.4 75.9 %psum.42 = f32[64]{0:T(128)S(1)} all-reduce(f32[64]{0:T(128)S(1)} %get-tuple-element.15), channel_id=1, replica_groups=mesh['train'=32,'cand'=8] {'train','cand'}, use_global_device_ids=true, to_apply=%region_3.0 | all-reduce | flops 64 | bytes 512 | tf_op jit(solution)/shard_map/psum | solution.py:65
  913.3 73.6 %psum.45 = f32[64]{0:T(128)S(1)} all-reduce(f32[64]{0:T(128)S(1)} %multiply_reduce_fusion.1), channel_id=1, replica_groups=mesh['train'=32,'cand'=8] {'train','cand'}, use_global_device_ids=true, to_apply=%region_10.0 | all-reduce | flops 64 | bytes 512 | tf_op jit(solution)/shard_map/psum | solution.py:65
  987.8 2.2 exponential_convert_fusion
  990.0 695.8 %all-gather.5.cloned.1.call-done = bf16[16384,64]{1,0:T(8,128)(2,1)} async-done(((bf16[64,64]{1,0:T(8,128)(2,1)}), bf16[16384,64]{1,0:T(8,128)(2,1)}) %all-gather.5.cloned.1.call-update) | async-done | bytes 2097168 | tf_op jit(solution)/shard_map/all_gather | solution.py:75
  1685.8 1.7 fusion.30
  1689.1 1.5 convolution_add_fusion.3
  1690.6 1.6 fusion.26
  1692.2 17.7 psum.46
  1709.8 65.0 %psum.47 = f32[64]{0:T(128)S(1)} all-reduce(f32[64]{0:T(128)S(1)} %psum.46), channel_id=1, replica_groups=mesh['train'=32,'cand'=8] {'train'}, use_global_device_ids=true, to_apply=%region_13.14 | all-reduce | flops 64 | bytes 512 | tf_op jit(solution)/shard_map/psum | solution.py:14
  1775.5 28.5 %all_gather.19 = bf16[512,64]{1,0:T(8,128)(2,1)S(1)} all-gather(bf16[64,64]{1,0:T(8,128)(2,1)S(1)} %get-tuple-element.16), channel_id=1, replica_groups=mesh['train'=32,'cand'=8] {'cand'}, dimensions={0}, use_global_device_ids=true | all-gather | bytes 73728 | tf_op jit(solution)/shard_map/all_gather | solution.py:95
  1805.2 2.7 fusion.21
  1807.9 109.2 %reduce-scatter.2.cloned.1.call-done = f32[32,64]{1,0:T(8,128)} async-done(((f32[1024,64]{1,0:T(8,128)}), f32[32,64]{1,0:T(8,128)}) %reduce-scatter.2.cloned.1.call-update) | async-done | bytes 8208 | tf_op jit(solution)/shard_map/reduce_scatter | solution.py:97
  1917.1 1.6 convolution_add_fusion.8
  (33 shorter events, 10.7 us)
Async XLA Ops:
  7.2 27.7 %copy-start = (f32[8,4096]{1,0:T(8,128)S(1)}, f32[8,4096]{1,0:T(8,128)}, u32[]{:S(2)}) copy-start(f32[8,4096]{1,0:T(8,128)} %param.11) | copy-start | bytes 393220
  7.2 82.7 %copy-start.1 = (f32[8,512]{1,0:T(8,128)S(1)}, f32[8,512]{1,0:T(8,128)}, u32[]{:S(2)}) copy-start(f32[8,512]{1,0:T(8,128)} %param.7) | copy-start | bytes 49156
  7.2 741.3 %all-gather.3.cloned.1.call-start = ((), (), s32[]{:S(2)}) async-start(), calls=%async_computation.1 | async-start | bytes 4210688 | tf_op jit(solution)/shard_map/all_gather | solution.py:75
  42.1 1643.8 %all-gather.5.cloned.1.call-start = ((), (), s32[]{:S(2)}) async-start(), calls=%async_computation.2 | async-start | bytes 4210688 | tf_op jit(solution)/shard_map/all_gather | solution.py:75
  92.4 895.4 %copy-start.3 = (f32[8,1024]{1,0:T(8,128)S(1)}, f32[8,1024]{1,0:T(8,128)}, u32[]{:S(2)}) copy-start(f32[8,1024]{1,0:T(8,128)} %param.8) | copy-start | bytes 98308
  93.7 659.5 %copy-start.4 = (bf16[64,4096]{1,0:T(8,128)(2,1)}, bf16[64,4096]{1,0:T(8,128)(2,1)S(1)}, u32[]{:S(2)}) copy-start(bf16[64,4096]{1,0:T(8,128)(2,1)S(1)} %fusion.18) | copy-start | bytes 1572868
  987.5 929.6 %reduce-scatter.2.cloned.1.call-start = ((), (), s32[]{:S(2)}) async-start(), calls=%async_computation.3 | async-start | bytes 540672 | tf_op jit(solution)/shard_map/reduce_scatter | solution.py:97
  990.0 815.2 %copy-start.2 = (f32[4096]{0:T(1024)S(1)}, f32[4096]{0:T(1024)}, u32[]{:S(2)}) copy-start(f32[4096]{0:T(1024)} %param.12) | copy-start | bytes 49156
Sparse Core Ops, SparseCore 0:
  42.2 706.2 all-gather.2
  987.6 698.1 all-gather.4
  1805.3 111.7 reduce-scatter.1

commit v2 on v0

--- a/solution.py
+++ b/solution.py
@@ -72,7 +72,9 @@
                 tile, piece[offset : offset + count], preferred_element_type=jnp.float32
             )
         image = total + noise_level * direction
-        curve = lax.psum(jnp.sum(direction * image, axis=0), ("train", "cand"))
+        own = jnp.sum(direction * image, axis=0)
+        blocks = lax.all_gather(own, ("train", "cand"))
+        curve = jnp.sum(blocks, axis=0)
         alpha = norm_now / curve
         solution = solution + alpha * direction
         residual = residual - alpha * image

time: 1850 us -> 2170 us (1.17)
  waiting for transfers between devices: 1460 us -> 1860 us
  blocking collectives: 336 us -> 255 us
    unnamed x3 -> x7, waiting for transfers between devices: 0.05 us -> 398 us
    psum x1 -> x0, blocking collectives: 82.4 us -> none  [body(): curve = lax.psum(jnp.sum(direction * image, axis=0), ('train', 'cand'))]
  transfers between devices with their start and end apart: 3 -> 5, of which waited for: 3 -> 5; matrix products, arithmetic and copies ran while one was open for 1% -> 1% of each run, Pallas kernels for 0% -> 0%
where the time goes in v2:
time: 2170 us
  waiting for transfers between devices  1860 us (86%)
  blocking collectives  255 us (12%)
  matrix products  32.9 us (2%)
    all_gather x2, waiting for transfers between devices, body(): piece = lax.all_gather(packed, ('train', 'cand'), axis=0, tiled=True)  1350 us
    unnamed x7, waiting for transfers between devices  398 us
    psum x2, blocking collectives, squares(): return lax.psum(jnp.sum(values * values, axis=0), ('train', 'cand'))  157 us
    reduce_scatter x1, waiting for transfers between devices, body(): lax.psum_scatter(kernel_rows(x_cand, x_train, train_norms, block_weights)...  111 us
    all_gather x1, blocking collectives, body(): column_points = lax.all_gather(x_train, 'train', axis=1, tiled=True)  44.9 us
  transfers between devices with their start and end apart: 5, of which 5 were waited for; matrix products, arithmetic and copies ran while one was open for 1% of the time, Pallas kernels for 0%

profile of v2, /device:TPU:4, one launch (start us, length us, event | category | flops | bytes accessed | tf_op | source)
XLA Modules:
  0.0 2170.0 jit_solution(6230876157154317989)
XLA Ops:
  7.2 27.6 %all_gather.27 = bf16[4096,64]{0,1:T(8,128)(2,1)S(1)} all-gather(bf16[512,64]{0,1:T(8,128)(2,1)} %param.13), channel_id=1, replica_groups=mesh['train'=32,'cand'=8] {'cand'}, dimensions={0}, use_global_device_ids=true | all-gather | bytes 589824 | tf_op jit(solution)/shard_map/all_gather | solution.py:44
  34.9 5.5 fusion.14
  40.3 1.7 fusion.56
  42.9 44.9 %all_gather.28 = f32[8,16384]{1,0:T(8,128)S(1)} all-gather(f32[8,512]{1,0:T(8,128)} %param.7), channel_id=1, replica_groups=mesh['train'=32,'cand'=8] {'train'}, dimensions={1}, use_global_device_ids=true | all-gather | bytes 540672 | tf_op jit(solution)/shard_map/all_gather | solution.py:49
  88.0 1.9 fusion.15
  93.7 654.8 %all-gather.5.cloned.1.call-done = bf16[16384,64]{1,0:T(8,128)(2,1)} async-done(((bf16[64,64]{1,0:T(8,128)(2,1)}), bf16[16384,64]{1,0:T(8,128)(2,1)}) %all-gather.5.cloned.1.call-update) | async-done | bytes 2097168 | tf_op jit(solution)/shard_map/all_gather | solution.py:65
  748.5 1.5 fusion.35
  750.1 1.5 convolution_add_fusion.7
  751.6 1.5 convolution_add_fusion.6
  753.2 1.6 multiply_reduce_fusion.2
  755.7 82.9 %psum.14 = f32[64]{0:T(128)S(1)} all-reduce(f32[64]{0:T(128)S(1)} %get-tuple-element.15), channel_id=1, replica_groups=mesh['train'=32,'cand'=8] {'train','cand'}, use_global_device_ids=true, to_apply=%region_3.0 | all-reduce | flops 64 | bytes 512 | tf_op jit(solution)/shard_map/psum | solution.py:55
  838.6 158.7 %all-reduce.5.cloned.1.call-done = f32[16384]{0:T(1024)} async-done(((f32[16384]{0:T(1024)}), f32[16384]{0:T(1024)}) %all-reduce.5.cloned.1.call-update) | async-done | bytes 65552
  998.3 74.2 %psum.15 = f32[64]{0:T(128)S(1)} all-reduce(f32[64]{0:T(128)S(1)} %multiply_reduce_fusion.1), channel_id=1, replica_groups=mesh['train'=32,'cand'=8] {'train','cand'}, use_global_device_ids=true, to_apply=%region_9.0 | all-reduce | flops 64 | bytes 512 | tf_op jit(solution)/shard_map/psum | solution.py:55
  1073.3 697.9 %all-gather.7.cloned.1.call-done = bf16[16384,64]{1,0:T(8,128)(2,1)} async-done(((bf16[64,64]{1,0:T(8,128)(2,1)}), bf16[16384,64]{1,0:T(8,128)(2,1)}) %all-gather.7.cloned.1.call-update) | async-done | bytes 2097168 | tf_op jit(solution)/shard_map/all_gather | solution.py:65
  1771.2 1.5 fusion.30
  1772.8 1.5 convolution_add_fusion.4
  1774.3 1.5 convolution_add_fusion.3
  1775.9 1.6 fusion.26
  1778.6 2.2 exponential_convert_fusion
  1780.8 239.0 %all-reduce.7.cloned.1.call-done = f32[16384]{0:T(1024)} async-done(((f32[16384]{0:T(1024)}), f32[16384]{0:T(1024)}) %all-reduce.7.cloned.1.call-update) | async-done | bytes 65552
  2021.4 25.1 %all_gather.35 = bf16[512,64]{1,0:T(8,128)(2,1)S(1)} all-gather(bf16[64,64]{1,0:T(8,128)(2,1)S(1)} %get-tuple-element.16), channel_id=1, replica_groups=mesh['train'=32,'cand'=8] {'cand'}, dimensions={0}, use_global_device_ids=true | all-gather | bytes 73728 | tf_op jit(solution)/shard_map/all_gather | solution.py:87
  2047.8 2.7 fusion.21
  2050.5 111.4 %reduce-scatter.2.cloned.1.call-done = f32[32,64]{1,0:T(8,128)} async-done(((f32[1024,64]{1,0:T(8,128)}), f32[32,64]{1,0:T(8,128)}) %reduce-scatter.2.cloned.1.call-update) | async-done | bytes 8208 | tf_op jit(solution)/shard_map/reduce_scatter | solution.py:89
  2161.9 1.6 convolution_add_fusion.8
  (45 shorter events, 11.5 us)
Async XLA Ops:
  7.2 27.7 %copy-start = (f32[8,4096]{1,0:T(8,128)S(1)}, f32[8,4096]{1,0:T(8,128)}, u32[]{:S(2)}) copy-start(f32[8,4096]{1,0:T(8,128)} %param.11) | copy-start | bytes 393220
  7.2 82.7 %copy-start.3 = (f32[8,512]{1,0:T(8,128)S(1)}, f32[8,512]{1,0:T(8,128)}, u32[]{:S(2)}) copy-start(f32[8,512]{1,0:T(8,128)} %param.7) | copy-start | bytes 49156
  7.2 741.3 %all-gather.5.cloned.1.call-start = ((), (), s32[]{:S(2)}) async-start(), calls=%async_computation.1 | async-start | bytes 4210688 | tf_op jit(solution)/shard_map/all_gather | solution.py:65
  42.1 955.3 %all-reduce.5.cloned.1.call-start = ((), (), s32[]{:S(2)}) async-start(), calls=%async_computation.4 | async-start | bytes 131072
  92.4 980.9 %copy-start.5 = (f32[8,1024]{1,0:T(8,128)S(1)}, f32[8,1024]{1,0:T(8,128)}, u32[]{:S(2)}) copy-start(f32[8,1024]{1,0:T(8,128)} %param.8) | copy-start | bytes 98308
  755.0 0.6 copy-start.2
  755.7 1015.6 %all-gather.7.cloned.1.call-start = ((), (), s32[]{:S(2)}) async-start(), calls=%async_computation.2 | async-start | bytes 4210688 | tf_op jit(solution)/shard_map/all_gather | solution.py:65
  1073.2 946.6 %all-reduce.7.cloned.1.call-start = ((), (), s32[]{:S(2)}) async-start(), calls=%async_computation.5 | async-start | bytes 131072
  1774.3 273.4 %copy-start.4 = (f32[4096]{0:T(1024)S(1)}, f32[4096]{0:T(1024)}, u32[]{:S(2)}) copy-start(f32[4096]{0:T(1024)} %param.12) | copy-start | bytes 49156
  1777.7 0.6 copy-start.1
  1778.4 383.5 %reduce-scatter.2.cloned.1.call-start = ((), (), s32[]{:S(2)}) async-start(), calls=%async_computation.3 | async-start | bytes 540672 | tf_op jit(solution)/shard_map/reduce_scatter | solution.py:89
Sparse Core Ops, SparseCore 0:
  42.2 706.2 all-gather.4
  755.8 241.5 all-reduce.4
  1073.4 697.8 all-gather.6
  1778.5 241.2 all-reduce.6
  2047.9 113.9 reduce-scatter.1
